TPU v7x, 32 devices: a whole 2x2x4 slice. The times are simulated.
32 devices in a mesh: tm: 4 (over y, x), space: 8 (over z, core).
Axes of the slice: x: 2, y: 2, z: 4, core: 2. Of those that a mesh axis runs over, the one named last changes fastest.
Arguments:
- video: bfloat16 [16, 16, 24, 3072], P('tm', 'space'), may hold values from -6 to 6
- w_qkv: bfloat16 [3072, 8, 384], P(None, 'space'), may hold values from -0.109375 to 0.109375
- w_out: bfloat16 [8, 128, 3072], P('space'), may hold values from -0.5 to 0.5
- q_gain: float32 [128], replicated, may hold values from 1 to 8
- k_gain: float32 [128], replicated, may hold values from 1 to 8
- tile_perm: int32 [4, 1536], P('tm'), may hold values from 0 to 1535, as said below
- window: int32 [6, 6], replicated, may hold values from 0 to 5, as said below
Outputs:
- mixed: bfloat16 [4, 1536, 3072], P('tm', 'space')
Inputs may be any that keep to these rules, and one draw needn't show every extreme that they name: `tile_perm`: each row is a permutation of the slots of one frame group in which slots t*256 to t*256 + 255 hold exactly the tokens of tile t; tile t covers frames of the group, rows (t // 3) * 8 onward and columns (t % 3) * 8 onward, 8 and 8 of them. `window`: row t holds 6 different tiles, the first being t.
All inputs are finite; a program needn't handle non-finite values.
Results may differ from a plain program's by a relative error of at most 0.023.
The roundings to bfloat16 on the way count: a program that leaves them out, or rounds other values in their place, can miss the bound.
Values may be sent and summed in bfloat16 or wider, within the bound.
A program may use at most 128 MiB of HBM per device.

v0:
```python
import jax
import jax.numpy as jnp
from jax import lax
from jax.sharding import PartitionSpec as P

TT = 4
TH = 8
TW = 8


def extended(cells, sides, width):
    for axis, dim in sides:
        count = lax.axis_size(axis)
        ends = count - 1
        head = lax.slice_in_dim(cells, 0, width, axis=dim)
        tail = lax.slice_in_dim(cells, cells.shape[dim] - width, cells.shape[dim], axis=dim)
        cells = jnp.concatenate(
            [
                lax.ppermute(tail, axis, [(i, (i + 1) % count) for i in range(ends)]),
                cells,
                lax.ppermute(head, axis, [((i + 1) % count, i) for i in range(ends)]),
            ],
            axis=dim,
        )
    return cells


def head_norm(values, gain):
    wide = values.astype(jnp.float32)
    scaled = wide * lax.rsqrt(jnp.mean(wide * wide, axis=-1, keepdims=True) + 1e-06)
    return (scaled * gain).astype(jnp.bfloat16)


def attend(queries, chosen, valid):
    heads_here = queries.shape[1]
    head_dim = queries.shape[2]
    span = chosen.shape[1] * chosen.shape[2]
    keys = chosen[:, :, :, :, 0, :].reshape(-1, heads_here, head_dim)
    values = chosen[:, :, :, :, 1, :].reshape(-1, heads_here, head_dim)
    scores = jnp.einsum(
        "qhd,khd->hqk", queries, keys, preferred_element_type=jnp.float32
    ) * head_dim ** (-0.5)
    live = jnp.repeat(valid, span)
    scores = jnp.where(live[None, None, :], scores, -jnp.inf)
    highest = jnp.max(scores, axis=-1, keepdims=True)
    weights = jnp.exp(scores - highest)
    probs = (weights / jnp.sum(weights, axis=-1, keepdims=True)).astype(jnp.bfloat16)
    result = jnp.einsum("hqk,khd->qhd", probs, values, preferred_element_type=jnp.float32)
    return result.astype(jnp.bfloat16)


def per_device(video, w_qkv, w_out, q_gain, k_gain, tile_perm, window):
    frames_here = video.shape[0]
    cols_here = video.shape[2]
    model_dim = video.shape[3]
    heads_here = w_qkv.shape[1]
    head_dim = w_out.shape[1]
    flat_w = w_qkv.reshape(model_dim, heads_here * 3 * head_dim)
    qkv = jnp.einsum(
        "frwd,dc->frwc",
        lax.all_gather(video, "space", axis=1, tiled=True),
        flat_w,
        preferred_element_type=jnp.float32,
    ).astype(jnp.bfloat16)
    group_tokens = frames_here * qkv.shape[1] * cols_here
    qkv = qkv.reshape(group_tokens, heads_here, 3, head_dim)
    ordered = jnp.take(qkv, tile_perm[0], axis=0)
    queries = head_norm(ordered[:, :, 0, :], q_gain)
    keys = head_norm(ordered[:, :, 1, :], k_gain)
    pairs = jnp.stack([keys, ordered[:, :, 2, :]], axis=2)
    beside_all = extended(pairs[None], (("tm", 0),), 1)
    tile_tokens = TT * TH * TW
    tile_count = group_tokens // tile_tokens
    beside_all = beside_all.reshape(3, tile_count, tile_tokens, heads_here, 2, head_dim)
    position = lax.axis_index("tm")
    valid = jnp.stack([position > 0, position >= 0, position < lax.axis_size("tm") - 1])
    query_tiles = queries.reshape(tile_count, tile_tokens, heads_here, head_dim)

    def one_tile(item):
        block, picks = item
        return attend(block, jnp.take(beside_all, picks, axis=1), valid)

    attn = lax.map(one_tile, (query_tiles, window)).reshape(group_tokens, heads_here, head_dim)
    flat_attn = attn.reshape(group_tokens, heads_here * head_dim)
    flat_out = w_out.reshape(heads_here * head_dim, model_dim)
    product = jnp.dot(flat_attn, flat_out, preferred_element_type=jnp.float32)
    summed = lax.psum_scatter(
        lax.optimization_barrier(product.astype(jnp.bfloat16))
        .astype(jnp.float32)
        .astype(jnp.bfloat16),
        "space",
        scatter_dimension=0,
        tiled=True,
    )
    return summed[None]


def solution(mesh):
    in_specs = (
        P("tm", "space", None, None),
        P(None, "space", None),
        P("space", None, None),
        P(),
        P(),
        P("tm", None),
        P(),
    )
    out_specs = P("tm", "space", None)
    return jax.shard_map(
        per_device, mesh=mesh, in_specs=in_specs, out_specs=out_specs, check_vma=False
    )
```

profile of v0, /device:TPU:5, one launch (start us, length us, event | category | flops | bytes accessed | tf_op | source)
XLA Modules:
  0.0 337.0 jit_solution(15814440508178612094)
XLA Ops:
  8.8 92.6 %all-gather.2.cloned.1.call-done = bf16[4,16,24,3072]{3,2,1,0:T(8,128)(2,1)} async-done(((bf16[4,2,24,3072]{3,2,1,0:T(8,128)(2,1)}), bf16[4,16,24,3072]{3,2,1,0:T(8,128)(2,1)}) %all-gather.2.cloned.1.call-update) | async-done | bytes 9437200 | tf_op jit(solution)/shard_map/all_gather | solution.py:61
  101.4 7.8 %fusion.11 = bf16[4,16,24,384]{3,2,1,0:T(8,128)(2,1)S(1)} fusion(bf16[4,16,24,3072]{3,2,1,0:T(8,128)(2,1)} %all-gather.2.cloned.1.call-done, bf16[3072,1,384]{2,0,1:T(8,128)(2,1)S(1)} %copy-done), kind=kOutput, calls=%fused_computation.25 | convolution fusion | flops 3624468480 | bytes 12976128 | tf_op jit(solution)/shard_map/frwd,dc->frwc/dot_general | solution.py:59
  109.1 1.8 reshape.274
  111.0 5.9 %gather_fusion.1 = bf16[1536,3,128]{2,1,0:T(4,128)(2,1)} fusion(bf16[1536,3,128]{2,1,0:T(4,128)(2,1)} %reshape.274, s32[2048]{0:T(1024)S(1)} %pad_clamp_fusion.1), kind=kCustom, calls=%fused_computation.1 | custom fusion | bytes 2365440 | tf_op jit(solution)/shard_map/jit(_take)/gather | solution.py:67
  116.8 1.7 bitcast_select_fusion.1
  121.3 3.1 collective-permute-start.1
  124.4 3.3 collective-permute-start
  127.7 1.4 multiply_convert_fusion
  129.1 13.2 %collective-permute-done.1 = bf16[1,1536,1,2,128]{4,1,3,2,0:T(8,128)(2,1)} collective-permute-done((bf16[1,1536,1,2,128]{4,1,3,2,0:T(8,128)(2,1)}, bf16[1,1536,1,2,128]{4,1,3,2,0:T(8,128)(2,1)}, u32[]{:S(2)}, u32[]{:S(2)}) %collective-permute-start.1) | collective-permute-done | bytes 786464 | tf_op jit(solution)/shard_map/ppermute | solution.py:21
  142.3 16.9 %collective-permute-done = bf16[1,1536,1,2,128]{4,1,3,2,0:T(8,128)(2,1)} collective-permute-done((bf16[1,1536,1,2,128]{4,1,3,2,0:T(8,128)(2,1)}, bf16[1,1536,1,2,128]{4,1,3,2,0:T(8,128)(2,1)}, u32[]{:S(2)}, u32[]{:S(2)}) %collective-permute-start) | collective-permute-done | bytes 786464 | tf_op jit(solution)/shard_map/ppermute | solution.py:19
  159.2 1.6 pad_maximum_fusion
  160.8 1.6 copy.36
  162.4 65.2 %while.10 = (s32[]{:T(128)}, bf16[6,256,1,128]{3,1,0,2:T(8,128)(2,1)S(1)}, s32[6,6]{1,0:T(8,128)}, bf16[3,6,256,1,2,128]{5,2,4,1,0,3:T(8,128)(2,1)}, pred[3]{0:T...) while((s32[]{:T(128)}, bf16[6,256,1,128]{3,1,0,2:T(8,128)(2,1)S(1)}, s32[6,6]{1,0:T(8,128)}, ...), condition=%wide.region_5.6_spmd, body=%wide.region_2.0_spmd.sunk | while | flops 614629952 | bytes 35811052 | solution.py:83
  163.9 4.0 %gather_fusion = bf16[6,3,256,2,128]{4,2,3,1,0:T(8,128)(2,1)} fusion(bf16[3,6,256,2,128]{4,2,3,1,0:T(8,128)(2,1)} %bitcast.82, s32[1024]{0:T(1024)S(1)} %pad_clamp_fusion.3), kind=kCustom, calls=%fused_computation.clone.1 | custom fusion | bytes 4718616 | tf_op jit(solution)/shard_map/while/body/eval_jaxpr/jit(_take)/gather | solution.py:81
  167.9 2.0 bitcast_select_fusion.3
  174.8 4.0 %gather_fusion = bf16[6,3,256,2,128]{4,2,3,1,0:T(8,128)(2,1)} fusion(bf16[3,6,256,2,128]{4,2,3,1,0:T(8,128)(2,1)} %bitcast.82, s32[1024]{0:T(1024)S(1)} %pad_clamp_fusion.3), kind=kCustom, calls=%fused_computation.clone.1 | custom fusion | bytes 4718616 | tf_op jit(solution)/shard_map/while/body/eval_jaxpr/jit(_take)/gather | solution.py:81
  178.8 2.0 bitcast_select_fusion.3
  182.8 1.1 fusion.39
  185.6 4.0 %gather_fusion = bf16[6,3,256,2,128]{4,2,3,1,0:T(8,128)(2,1)} fusion(bf16[3,6,256,2,128]{4,2,3,1,0:T(8,128)(2,1)} %bitcast.82, s32[1024]{0:T(1024)S(1)} %pad_clamp_fusion.3), kind=kCustom, calls=%fused_computation.clone.1 | custom fusion | bytes 4718616 | tf_op jit(solution)/shard_map/while/body/eval_jaxpr/jit(_take)/gather | solution.py:81
  189.6 2.0 bitcast_select_fusion.3
  193.7 1.1 fusion.39
  196.5 4.0 %gather_fusion = bf16[6,3,256,2,128]{4,2,3,1,0:T(8,128)(2,1)} fusion(bf16[3,6,256,2,128]{4,2,3,1,0:T(8,128)(2,1)} %bitcast.82, s32[1024]{0:T(1024)S(1)} %pad_clamp_fusion.3), kind=kCustom, calls=%fused_computation.clone.1 | custom fusion | bytes 4718616 | tf_op jit(solution)/shard_map/while/body/eval_jaxpr/jit(_take)/gather | solution.py:81
  200.5 2.0 bitcast_select_fusion.3
  204.6 1.1 fusion.39
  207.4 4.0 %gather_fusion = bf16[6,3,256,2,128]{4,2,3,1,0:T(8,128)(2,1)} fusion(bf16[3,6,256,2,128]{4,2,3,1,0:T(8,128)(2,1)} %bitcast.82, s32[1024]{0:T(1024)S(1)} %pad_clamp_fusion.3), kind=kCustom, calls=%fused_computation.clone.1 | custom fusion | bytes 4718616 | tf_op jit(solution)/shard_map/while/body/eval_jaxpr/jit(_take)/gather | solution.py:81
  211.3 2.0 bitcast_select_fusion.3
  215.4 1.1 fusion.39
  218.2 4.0 %gather_fusion = bf16[6,3,256,2,128]{4,2,3,1,0:T(8,128)(2,1)} fusion(bf16[3,6,256,2,128]{4,2,3,1,0:T(8,128)(2,1)} %bitcast.82, s32[1024]{0:T(1024)S(1)} %pad_clamp_fusion.3), kind=kCustom, calls=%fused_computation.clone.1 | custom fusion | bytes 4718616 | tf_op jit(solution)/shard_map/while/body/eval_jaxpr/jit(_take)/gather | solution.py:81
  222.2 2.0 bitcast_select_fusion.3
  226.3 1.1 fusion.39
  227.6 6.2 %convolution_convert_fusion = bf16[1536,3072]{1,0:T(8,128)(2,1)} fusion(bf16[1536,128]{1,0:T(8,128)(2,1)S(1)} %bitcast.86, bf16[1,128,3072]{2,1,0:T(8,128)(2,1)} %param.11), kind=kOutput, calls=%fused_computation.21 | convolution fusion | flops 1212678144 | bytes 10616832 | tf_op jit(solution)/shard_map/dot_general | solution.py:86
  233.8 96.4 %reduce-scatter.2.cloned.1.call-done = bf16[192,3072]{1,0:T(8,128)(2,1)} async-done(((bf16[1536,3072]{1,0:T(8,128)(2,1)}), bf16[192,3072]{1,0:T(8,128)(2,1)}) %reduce-scatter.2.cloned.1.call-update) | async-done | bytes 1179664 | tf_op jit(solution)/shard_map/reduce_scatter | solution.py:87
  (97 shorter events, 28.6 us)
Async XLA Ops:
  6.5 94.8 %copy-start = (bf16[3072,1,384]{2,0,1:T(8,128)(2,1)S(1)}, bf16[3072,1,384]{2,0,1:T(8,128)(2,1)}, u32[]{:S(2)}) copy-start(bf16[3072,1,384]{2,0,1:T(8,128)(2,1)} %param.10) | copy-start | bytes 7077892
  6.5 94.8 %all-gather.2.cloned.1.call-start = ((), (), s32[]{:S(2)}) async-start(), calls=%async_computation.1 | async-start | bytes 10616832 | tf_op jit(solution)/shard_map/all_gather | solution.py:61
  7.3 322.9 %reduce-scatter.2.cloned.1.call-start = ((), (), s32[]{:S(2)}) async-start(), calls=%async_computation.2 | async-start | bytes 10616832 | tf_op jit(solution)/shard_map/reduce_scatter | solution.py:87
  116.8 3.2 copy-start.3
  119.0 8.7 %copy-start.2 = (f32[128]{0:T(128)S(1)}, f32[128]{0:T(128)}, u32[]{:S(2)}) copy-start(f32[128]{0:T(128)} %param.12) | copy-start | bytes 1540
  121.3 21.1 %collective-permute-start.1 = (bf16[1,1536,1,2,128]{4,1,3,2,0:T(8,128)(2,1)}, bf16[1,1536,1,2,128]{4,1,3,2,0:T(8,128)(2,1)}, u32[]{:S(2)}, u32[]{:S(2)}) collective-permute-start(bf16[1,1536,1,2,128]{4,1,3,2,0:T(8,128)(2,1)} %get-tuple-element.59), channel_id=1, source_target_pairs={{8,0},{16,8},{24,16},{9,1},{17,9},{25,17},{10,2},{18,10},{26,18},{... | collective-permute-start | bytes 2359304 | tf_op jit(solution)/shard_map/ppermute | solution.py:21
  124.4 34.8 %collective-permute-start = (bf16[1,1536,1,2,128]{4,1,3,2,0:T(8,128)(2,1)}, bf16[1,1536,1,2,128]{4,1,3,2,0:T(8,128)(2,1)}, u32[]{:S(2)}, u32[]{:S(2)}) collective-permute-start(bf16[1,1536,1,2,128]{4,1,3,2,0:T(8,128)(2,1)} %get-tuple-element.59), channel_id=1, source_target_pairs={{0,8},{8,16},{16,24},{1,9},{9,17},{17,25},{2,10},{10,18},{18,26},{... | collective-permute-start | bytes 2359304 | tf_op jit(solution)/shard_map/ppermute | solution.py:19
  160.8 1.6 copy-start.1
Sparse Core Ops, SparseCore 0:
  9.0 92.3 all-gather.1
  233.9 96.2 reduce-scatter.1
where the time goes:
time: 342 us; the launch traced here: 337 us
  waiting for transfers between devices  220 us (64%)
  local copies, waits for them, and re-layouts  37.2 us (11%)
  other arithmetic  33.8 us (10%)
  matrix products  26 us (8%)
  between operations  13.5 us (4%)
  starting transfers between devices  6.38 us (2%)
    reduce_scatter x1, waiting for transfers between devices, per_device(): lax.psum_scatter(lax.optimization_barrier(product.astype(jnp.bfloat16)).a...  96.4 us
    all_gather x1, waiting for transfers between devices, per_device(): lax.all_gather(video, 'space', axis=1, tiled=True)  92.6 us
    gather x6, local copies, waits for them, and re-layouts, one_tile(): return attend(block, jnp.take(beside_all, picks, axis=1), valid)  23.9 us
    ppermute x1, waiting for transfers between devices, extended(): lax.ppermute(tail, axis, [(i, (i + 1) % count) for i in range(ends)])  16.9 us
    select_n x12, other arithmetic, one_tile(): return attend(block, jnp.take(beside_all, picks, axis=1), valid)  15.9 us
    ppermute x1, waiting for transfers between devices, extended(): lax.ppermute(head, axis, [((i + 1) % count, i) for i in range(ends)])  13.2 us
    dot_general x1, matrix products, per_device(): jnp.einsum('frwd,dc->frwc', lax.all_gather(video, 'space', axis=1, tiled=...  7.77 us
  transfers between devices with their start and end apart: 4, of which 4 were waited for; matrix products, arithmetic and copies ran while one was open for 1% of the time, Pallas kernels for 0%

commit v1 on v0

--- a/solution.py
+++ b/solution.py
@@ -1,11 +1,402 @@
+import functools
+import math
+
 import jax
 import jax.numpy as jnp
 from jax import lax
+from jax.experimental import pallas as pl
+from jax.experimental.pallas import tpu as pltpu
 from jax.sharding import PartitionSpec as P
 
+MESH = pl.DeviceIdType.MESH
 TT = 4
 TH = 8
 TW = 8
+
+
+def fused_kernel(
+    n_tm,
+    n_z,
+    x_ref,
+    wq_ref,
+    wo_ref,
+    qg_ref,
+    kg_ref,
+    pos_ref,
+    out_ref,
+    xg,
+    wall,
+    queries,
+    kv,
+    scores,
+    attn,
+    attn_in,
+    part_out,
+    part_in,
+    wz_send,
+    wz_recv,
+    wt_send,
+    wt_recv,
+    x_send,
+    x_recv,
+    sib_send,
+    sib_recv,
+    kv_send,
+    kv_recv,
+    at_send,
+    at_recv,
+    pt_send,
+    pt_recv,
+):
+    tm = lax.axis_index("tm")
+    space = lax.axis_index("space")
+    z = space // 2
+    core = space % 2
+    sibling = z * 2 + 1 - core
+    tokens, model = x_ref.shape
+    shards = 2 * n_z
+    group = shards * tokens
+    hd = kv.shape[2] // 3
+    quarter = model // n_tm
+
+    def remote(src, dst, send, recv, t, s):
+        return pltpu.make_async_remote_copy(
+            src_ref=src, dst_ref=dst, send_sem=send, recv_sem=recv,
+            device_id=(t, s), device_id_type=MESH,
+        )
+
+    def rows_of(index, count):
+        return pl.ds(pl.multiple_of(index * count, count), count)
+
+    def w_ring(way, u, zz):
+        target = z + 1 if way == 0 else z - 1
+        block = wall.at[tm, rows_of(zz, hd)]
+        return remote(block, block, wz_send.at[way, u], wz_recv.at[way, u], tm, target * 2 + core)
+
+    def x_ring(way, u, zz):
+        target = z + 1 if way == 0 else z - 1
+        block = xg.at[zz * 2 + core]
+        return remote(block, block, x_send.at[way, u], x_recv.at[way, u], tm, target * 2 + core)
+
+    def w_peer(k, zz, owner):
+        block = wall.at[owner, rows_of(zz, hd)]
+        return remote(
+            block, block, wt_send.at[k - 1, zz], wt_recv.at[k - 1, zz], (tm + k) % n_tm, space
+        )
+
+    def x_sibling(zz, side):
+        block = xg.at[zz * 2 + side]
+        return remote(block, block, sib_send.at[zz], sib_recv.at[zz], tm, sibling)
+
+    def kv_copy(way, slot):
+        target = tm - 1 if way == 0 else tm + 1
+        rows = rows_of(slot, tokens)
+        return remote(
+            kv.at[0, rows, pl.ds(0, 2 * hd)],
+            kv.at[2 - way, rows, pl.ds(0, 2 * hd)],
+            kv_send.at[way, slot],
+            kv_recv.at[way, slot],
+            target,
+            space,
+        )
+
+    def attn_copy(zz):
+        return remote(
+            attn.at[zz], attn_in.at[z], at_send.at[zz], at_recv.at[z], tm, zz * 2 + core
+        )
+
+    def attn_arrival(zz):
+        return remote(
+            attn.at[zz], attn_in.at[zz], at_send.at[zz], at_recv.at[zz], tm, zz * 2 + core
+        )
+
+    def part_copy(j):
+        return remote(
+            part_out.at[j], part_in.at[j], pt_send.at[j], pt_recv.at[j], tm, sibling
+        )
+
+    barrier = pltpu.get_barrier_semaphore()
+    for k in range(1, n_z):
+        pl.semaphore_signal(
+            barrier, inc=1, device_id=(tm, (z + k) % n_z * 2 + core), device_id_type=MESH
+        )
+    for k in range(1, n_tm):
+        pl.semaphore_signal(barrier, inc=1, device_id=((tm + k) % n_tm, space), device_id_type=MESH)
+    pl.semaphore_signal(barrier, inc=1, device_id=(tm, sibling), device_id_type=MESH)
+    for j in range(n_tm):
+        wall[j, rows_of(z, hd), :] = wo_ref[:, j * quarter : (j + 1) * quarter]
+    xg[space] = x_ref[...]
+    kv[0, :, 2 * hd :] = jnp.ones((group, hd), jnp.bfloat16)
+    pl.semaphore_wait(barrier, n_z - 1 + n_tm - 1 + 1)
+
+    def norm(value, gain):
+        scaled = value * lax.rsqrt(jnp.mean(value * value, axis=-1, keepdims=True) + 1e-06)
+        return (scaled * gain).astype(jnp.bfloat16)
+
+    def project(slot):
+        rows = rows_of(slot, tokens)
+        qkv = jnp.dot(xg[slot], wq_ref[...], preferred_element_type=jnp.float32)
+        qkv = qkv.astype(jnp.bfloat16)
+        queries[rows, :] = norm(qkv[:, :hd].astype(jnp.float32), qg_ref[...])
+        kv[0, rows, 0:hd] = norm(qkv[:, hd : 2 * hd].astype(jnp.float32), kg_ref[...])
+        kv[0, rows, hd : 2 * hd] = qkv[:, 2 * hd :]
+
+    def inside(zz):
+        return jnp.logical_and(zz >= 0, zz < n_z)
+
+    def forwards(way):
+        return z < n_z - 1 if way == 0 else z > 0
+
+    def step(u, carry):
+        for way in (0, 1):
+            zz = z - u if way == 0 else z + u
+            live = inside(zz)
+
+            @pl.when(jnp.logical_and(live, u > 0))
+            def _():
+                w_ring(way, u - 1, zz).wait_recv()
+
+            @pl.when(jnp.logical_and(live, forwards(way)))
+            def _():
+                w_ring(way, u, zz).start()
+
+            @pl.when(jnp.logical_and(live, u > 0))
+            def _():
+                for k in range(1, n_tm):
+                    w_peer(k, zz, tm).start()
+
+        for way in (0, 1):
+            zz = z - u if way == 0 else z + u
+            live = inside(zz)
+            fresh = live if way == 0 else jnp.logical_and(live, u > 0)
+
+            @pl.when(jnp.logical_and(live, u > 0))
+            def _():
+                x_ring(way, u - 1, zz).wait_recv()
+
+            @pl.when(jnp.logical_and(live, forwards(way)))
+            def _():
+                x_ring(way, u, zz).start()
+
+            @pl.when(fresh)
+            def _():
+                x_sibling(zz, core).start()
+
+        def item(i, carry):
+            way = i % 2
+            other = i // 2
+            zz = z - u + way * 2 * u
+            fresh = jnp.logical_and(inside(zz), way * (1 - jnp.minimum(u, 1)) == 0)
+
+            @pl.when(fresh)
+            def _():
+                @pl.when(other == 1)
+                def _():
+                    x_sibling(zz, 1 - core).wait_recv()
+
+                slot = zz * 2 + core + other * (1 - 2 * core)
+                project(slot)
+
+                @pl.when(tm > 0)
+                def _():
+                    kv_copy(0, slot).start()
+
+                @pl.when(tm < n_tm - 1)
+                def _():
+                    kv_copy(1, slot).start()
+
+            return carry
+
+        lax.fori_loop(0, 4, item, 0)
+        return carry
+
+    lax.fori_loop(0, n_z, step, 0)
+
+    for way in (0, 1):
+        here = 2 - way
+        live = tm < n_tm - 1 if way == 0 else tm > 0
+
+        @pl.when(live)
+        def _():
+            kv[here, :, 2 * hd :] = jnp.ones((group, hd), jnp.bfloat16)
+
+            def arrive(slot, carry):
+                kv_copy(way, slot).wait_recv()
+                return carry
+
+            lax.fori_loop(0, shards, arrive, 0)
+
+        @pl.when(jnp.logical_not(live))
+        def _():
+            kv[here, :, 0:hd] = kv[0, :, 0:hd]
+            kv[here, :, hd:] = jnp.zeros((group, 2 * hd), jnp.bfloat16)
+
+    factor = math.log2(math.e) * hd**-0.5
+    block_rows = 2 * tokens
+
+    def attend_block(i, carry):
+        zz = (z + 1 + i) % n_z
+        pos = pos_ref[rows_of(zz, block_rows), :]
+        lanes = lax.broadcasted_iota(jnp.int32, (block_rows, group), 1)
+        pick = jnp.where(lanes == pos, 1.0, 0.0).astype(jnp.bfloat16)
+        query = jnp.dot(pick, queries[...], preferred_element_type=jnp.float32)
+        query = query.astype(jnp.bfloat16)
+        highest = None
+        for part in range(3):
+            score = lax.dot_general(
+                query,
+                kv[part, :, 0:hd],
+                (((1,), (1,)), ((), ())),
+                preferred_element_type=jnp.float32,
+            )
+            scores[part] = score
+            top = jnp.max(score, axis=-1, keepdims=True)
+            highest = top if highest is None else jnp.maximum(highest, top)
+        total = jnp.zeros((block_rows, 2 * hd), jnp.float32)
+        for part in range(3):
+            weights = jnp.exp2((scores[part] - highest) * factor).astype(jnp.bfloat16)
+            total += jnp.dot(weights, kv[part, :, hd:], preferred_element_type=jnp.float32)
+        result = (total[:, :hd] / total[:, hd:]).astype(jnp.bfloat16)
+
+        @pl.when(zz == z)
+        def _():
+            attn_in[z] = result
+
+        @pl.when(zz != z)
+        def _():
+            attn[zz] = result
+            attn_copy(zz).start()
+
+        return carry
+
+    lax.fori_loop(0, n_z, attend_block, 0)
+
+    def others(body):
+        for k in range(1, n_z):
+            body((z + k) % n_z)
+
+    def weights_in(zz):
+        for k in range(1, n_tm):
+            w_peer(k, zz, (tm + n_tm - k) % n_tm).wait_recv()
+
+    others(weights_in)
+    others(lambda zz: attn_arrival(zz).wait_recv())
+
+    def mixed(side, j):
+        rows = rows_of(side, tokens)
+        left = jnp.concatenate([attn_in[zz, rows, :] for zz in range(n_z)], axis=1)
+        return jnp.dot(left, wall[j], preferred_element_type=jnp.float32)
+
+    for j in range(n_tm):
+        part_out[j] = mixed(1 - core, j).astype(jnp.bfloat16)
+        part_copy(j).start()
+    for j in range(n_tm):
+        own = mixed(core, j)
+        part_copy(j).wait_recv()
+        total = own + part_in[j].astype(jnp.float32)
+        out_ref[:, j * quarter : (j + 1) * quarter] = total.astype(jnp.bfloat16)
+
+    for j in range(n_tm):
+        part_copy(j).wait_send()
+
+    def sent(zz):
+        attn_copy(zz).wait_send()
+        for k in range(1, n_tm):
+            w_peer(k, zz, tm).wait_send()
+
+    others(sent)
+
+    def drain(slot, carry):
+        @pl.when(tm > 0)
+        def _():
+            kv_copy(0, slot).wait_send()
+
+        @pl.when(tm < n_tm - 1)
+        def _():
+            kv_copy(1, slot).wait_send()
+
+        return carry
+
+    lax.fori_loop(0, shards, drain, 0)
+    for zz in range(n_z):
+        x_sibling(zz, core).wait_send()
+    for u in range(n_z - 1):
+        for way in (0, 1):
+            zz = z - u if way == 0 else z + u
+
+            @pl.when(jnp.logical_and(inside(zz), forwards(way)))
+            def _():
+                w_ring(way, u, zz).wait_send()
+                x_ring(way, u, zz).wait_send()
+
+
+def fused(n_tm, n_z, x, wq, wo, q_gain, k_gain, pos):
+    tokens, model = x.shape
+    hd = wo.shape[0]
+    shards = 2 * n_z
+    group = shards * tokens
+    bf = jnp.bfloat16
+    dma = pltpu.SemaphoreType.DMA
+    vmem = pl.BlockSpec(memory_space=pltpu.VMEM)
+    return pl.pallas_call(
+        functools.partial(fused_kernel, n_tm, n_z),
+        out_shape=jax.ShapeDtypeStruct((tokens, model), bf),
+        in_specs=[vmem] * 6,
+        out_specs=vmem,
+        scratch_shapes=[
+            pltpu.VMEM((shards, tokens, model), bf),
+            pltpu.VMEM((n_tm, n_z * hd, model // n_tm), bf),
+            pltpu.VMEM((group, hd), bf),
+            pltpu.VMEM((3, group, 3 * hd), bf),
+            pltpu.VMEM((3, 2 * tokens, group), jnp.float32),
+            pltpu.VMEM((n_z, 2 * tokens, hd), bf),
+            pltpu.VMEM((n_z, 2 * tokens, hd), bf),
+            pltpu.VMEM((n_tm, tokens, model // n_tm), bf),
+            pltpu.VMEM((n_tm, tokens, model // n_tm), bf),
+            dma((2, n_z)),
+            dma((2, n_z)),
+            dma((n_tm - 1, n_z)),
+            dma((n_tm - 1, n_z)),
+            dma((2, n_z)),
+            dma((2, n_z)),
+            dma((n_z,)),
+            dma((n_z,)),
+            dma((2, shards)),
+            dma((2, shards)),
+            dma((n_z,)),
+            dma((n_z,)),
+            dma((n_tm,)),
+            dma((n_tm,)),
+        ],
+        compiler_params=pltpu.CompilerParams(
+            collective_id=0, has_side_effects=True, vmem_limit_bytes=56 * 1024 * 1024
+        ),
+    )(x, wq, wo, q_gain, k_gain, pos)
+
+
+def whole_window(video, w_qkv, w_out, q_gain, k_gain, tile_perm):
+    frames, rows_here, cols, model = video.shape
+    n_tm = lax.axis_size("tm")
+    n_space = lax.axis_size("space")
+    hd = w_out.shape[1]
+    place = tile_perm[0]
+    rows = rows_here * n_space
+    frame = place // (rows * cols)
+    row = place // cols % rows
+    col = place % cols
+    tokens = frames * rows_here * cols
+    pos = (row // rows_here) * tokens + (frame * rows_here + row % rows_here) * cols + col
+    mixed = fused(
+        n_tm,
+        n_space // 2,
+        video.reshape(tokens, model),
+        w_qkv.reshape(model, 3 * hd),
+        w_out.reshape(hd, model),
+        q_gain.reshape(1, hd),
+        k_gain.reshape(1, hd),
+        pos.reshape(-1, 1),
+    )
+    return mixed[None]
 
 
 def extended(cells, sides, width):
@@ -50,6 +441,9 @@
 
 
 def per_device(video, w_qkv, w_out, q_gain, k_gain, tile_perm, window):
+    tiles = video.shape[0] * video.shape[1] * lax.axis_size("space") * video.shape[2] // (TT * TH * TW)
+    if window.shape[1] == tiles and w_qkv.shape[1] == 1:
+        return whole_window(video, w_qkv, w_out, q_gain, k_gain, tile_perm)
     frames_here = video.shape[0]
     cols_here = video.shape[2]
     model_dim = video.shape[3]

time: 342 us -> 143 us (0.42); the launches traced: 337 us -> 143 us
  waiting for transfers between devices: 220 us -> 0 us
  Pallas kernels: 0 us -> 135 us
  local copies, waits for them, and re-layouts: 37.2 us -> 4.02 us
  other arithmetic: 33.8 us -> 3.89 us
  matrix products: 26 us -> 0 us
  between operations: 13.5 us -> 0.05 us
  starting transfers between devices: 6.38 us -> 0 us
    pallas_call x0 -> x1, Pallas kernels: none -> 135 us  [fused(): pl.pallas_call(functools.partial(fused_kernel, n_tm, n_z), out_shape=jax....]
    reduce_scatter x1 -> x0, waiting for transfers between devices: 96.4 us -> none  [per_device(): lax.psum_scatter(lax.optimization_barrier(product.astype(jnp.bfloat16)).a...]
    all_gather x1 -> x0, waiting for transfers between devices: 92.6 us -> none  [per_device(): lax.all_gather(video, 'space', axis=1, tiled=True)]
    ppermute x2 -> x0, waiting for transfers between devices: 30.1 us -> none  [the longest x1 16.9 us: extended(): lax.ppermute(tail, axis, [(i, (i + 1) % count) for i in range(ends)])]
    gather x7 -> x0, local copies, waits for them, and re-layouts: 29.7 us -> none  [the longest x6 23.9 us: one_tile(): return attend(block, jnp.take(beside_all, picks, axis=1), valid)]
    dot_general x14 -> x0, matrix products: 26 us -> none  [the longest x1 7.77 us: per_device(): jnp.einsum('frwd,dc->frwc', lax.all_gather(video, 'space', axis=1, tiled=...]
    select_n x14 -> x0, other arithmetic: 18.3 us -> none  [the longest x12 15.9 us: one_tile(): return attend(block, jnp.take(beside_all, picks, axis=1), valid)]
    ppermute x2 -> x0, starting transfers between devices: 6.34 us -> none  [the longest x1 3.27 us: extended(): lax.ppermute(tail, axis, [(i, (i + 1) % count) for i in range(ends)])]
  transfers between devices with their start and end apart: 4 -> 0, of which waited for: 4 -> 0; matrix products, arithmetic and copies ran while one was open for 1% -> 0% of each run, Pallas kernels for 0% -> 0%
where the time goes in v1:
time: 143 us
  Pallas kernels  135 us (94%)
  local copies, waits for them, and re-layouts  4.02 us (3%)
  other arithmetic  3.89 us (3%)
    pallas_call x1, Pallas kernels, fused(): pl.pallas_call(functools.partial(fused_kernel, n_tm, n_z), out_shape=jax....  135 us

profile of v1, /device:TPU:5, one launch (start us, length us, event | category | flops | bytes accessed | tf_op | source)
XLA Modules:
  0.0 143.0 jit_solution(7998895567341717537)
XLA Ops:
  0.0 0.7 compare_bitcast_fusion
  0.7 0.7 divide_bitcast_fusion.1
  1.5 0.4 copy.24
  1.8 0.4 copy.19
  2.2 0.3 copy.20
  2.5 0.3 copy.18
  2.8 0.3 copy.25
  3.1 2.4 %fusion.3.pos_ref = s32[1536,1]{1,0:T(8,128)} fusion(s32[1536,1]{1,0:T(8,128)S(1)} %copy.25, s32[1536,1]{1,0:T(8,128)S(1)} %copy.18, pred[1536,1]{1,0:T(8,128)(4,1)S(1)} %copy.19, pred[1536,1]{1,0:T(8,128)(4,1)S(1)} %copy.24, s32[1536,1]{1,0:T(8,128)S(1)} %copy.20), kind=kLoop, calls=%fused_computation.14 | loop fusion | flops 72192 | bytes 27648 | tf_op jit(solution)/shard_map/add | solution.py:388
  5.6 135.0 %shard_map.64 = bf16[192,3072]{1,0:T(8,128)(2,1)} custom-call(bf16[192,3072]{1,0:T(8,128)(2,1)} %bitcast.18, bf16[3072,384]{1,0:T(8,128)(2,1)} %bitcast.17, bf16[128,3072]{1,0:T(8,128)(2,1)} %bitcast.19, f32[1,128]{1,0:T(1,128)} %bitcast.20, f32[1,128]{1,0:T(1,128)} %bitcast.21, s32[1536,1]{1,0:T(8,128)} %fusion.3.pos_ref), custom_call_target="tpu_custom_call" | custom-call | tf_op jit(solution)/shard_map/pallas_call | solution.py:341
  140.6 2.4 %copy.31 = bf16[1,192,3072]{2,1,0:T(8,128)(2,1)} copy(bf16[1,192,3072]{2,1,0:T(8,128)(2,1)} %bitcast.16) | data formatting | bytes 2359296

commit v2 on v1

--- a/solution.py
+++ b/solution.py
@@ -17,16 +17,19 @@
 def fused_kernel(
     n_tm,
     n_z,
+    frame,
     x_ref,
     wq_ref,
     wo_ref,
     qg_ref,
     kg_ref,
-    pos_ref,
+    perm_ref,
     out_ref,
     xg,
     wall,
-    queries,
+    inner_w,
+    stage,
+    place,
     kv,
     scores,
     attn,
@@ -47,6 +50,12 @@
     at_recv,
     pt_send,
     pt_recv,
+    wq_send,
+    wq_recv,
+    wp_send,
+    wp_recv,
+    qkv_send,
+    qkv_recv,
 ):
     tm = lax.axis_index("tm")
     space = lax.axis_index("space")
@@ -56,8 +65,12 @@
     tokens, model = x_ref.shape
     shards = 2 * n_z
     group = shards * tokens
-    hd = kv.shape[2] // 3
+    hd = kv.shape[2] // 4
     quarter = model // n_tm
+    inner = jnp.logical_and(z > 0, z < n_z - 1)
+    outer = jnp.logical_not(inner)
+    end_of = (z - 1) * (n_z - 1)
+    inner_of = 1 + z // (n_z - 1)
 
     def remote(src, dst, send, recv, t, s):
         return pltpu.make_async_remote_copy(
@@ -92,12 +105,34 @@
         target = tm - 1 if way == 0 else tm + 1
         rows = rows_of(slot, tokens)
         return remote(
-            kv.at[0, rows, pl.ds(0, 2 * hd)],
-            kv.at[2 - way, rows, pl.ds(0, 2 * hd)],
+            kv.at[0, rows, pl.ds(hd, 2 * hd)],
+            kv.at[2 - way, rows, pl.ds(hd, 2 * hd)],
             kv_send.at[way, slot],
             kv_recv.at[way, slot],
             target,
             space,
+        )
+
+    def wq_inward():
+        rows = rows_of(tm, quarter)
+        return remote(
+            wq_ref.at[rows], inner_w.at[rows], wq_send, wq_recv, tm, inner_of * 2 + core
+        )
+
+    def wq_peer(k, owner):
+        block = inner_w.at[rows_of(owner, quarter)]
+        return remote(
+            block, block, wp_send.at[k - 1], wp_recv.at[k - 1], (tm + k) % n_tm, space
+        )
+
+    def qkv_outward(slot):
+        return remote(
+            stage.at[slot],
+            kv.at[0, rows_of(slot, tokens), pl.ds(0, 3 * hd)],
+            qkv_send.at[slot],
+            qkv_recv.at[slot],
+            tm,
+            end_of * 2 + core,
         )
 
     def attn_copy(zz):
@@ -126,55 +161,82 @@
     for j in range(n_tm):
         wall[j, rows_of(z, hd), :] = wo_ref[:, j * quarter : (j + 1) * quarter]
     xg[space] = x_ref[...]
-    kv[0, :, 2 * hd :] = jnp.ones((group, hd), jnp.bfloat16)
+    kv[0, :, 3 * hd :] = jnp.ones((group, hd), jnp.bfloat16)
     pl.semaphore_wait(barrier, n_z - 1 + n_tm - 1 + 1)
+
+    @pl.when(outer)
+    def _():
+        wq_inward().start()
 
     def norm(value, gain):
         scaled = value * lax.rsqrt(jnp.mean(value * value, axis=-1, keepdims=True) + 1e-06)
         return (scaled * gain).astype(jnp.bfloat16)
 
-    def project(slot):
-        rows = rows_of(slot, tokens)
-        qkv = jnp.dot(xg[slot], wq_ref[...], preferred_element_type=jnp.float32)
+    def project(slot, weights):
+        qkv = jnp.dot(xg[slot], weights[...], preferred_element_type=jnp.float32)
         qkv = qkv.astype(jnp.bfloat16)
-        queries[rows, :] = norm(qkv[:, :hd].astype(jnp.float32), qg_ref[...])
-        kv[0, rows, 0:hd] = norm(qkv[:, hd : 2 * hd].astype(jnp.float32), kg_ref[...])
-        kv[0, rows, hd : 2 * hd] = qkv[:, 2 * hd :]
+        query = norm(qkv[:, :hd].astype(jnp.float32), qg_ref[...])
+        key = norm(qkv[:, hd : 2 * hd].astype(jnp.float32), kg_ref[...])
+        return jnp.concatenate([query, key, qkv[:, 2 * hd :]], axis=1)
 
     def inside(zz):
         return jnp.logical_and(zz >= 0, zz < n_z)
 
-    def forwards(way):
+    def forwards_w(way):
         return z < n_z - 1 if way == 0 else z > 0
+
+    def forwards_x(way):
+        return z < n_z - 2 if way == 0 else z > 1
+
+    def spread_w(u):
+        for way in (0, 1):
+            zz = z - u if way == 0 else z + u
+            live = inside(zz)
+
+            @pl.when(jnp.logical_and(live, u > 0))
+            def _():
+                w_ring(way, u - 1, zz).wait_recv()
+
+            @pl.when(jnp.logical_and(live, forwards_w(way)))
+            def _():
+                w_ring(way, u, zz).start()
+
+            @pl.when(jnp.logical_and(live, u > 0))
+            def _():
+                for k in range(1, n_tm):
+                    w_peer(k, zz, tm).start()
+
+    def pick_item(u, i):
+        way = i % 2
+        other = i // 2
+        zz = z - u + way * 2 * u
+        fresh = jnp.logical_and(inside(zz), way * (1 - jnp.minimum(u, 1)) == 0)
+        return zz, other, zz * 2 + core + other * (1 - 2 * core), fresh
+
+    def outward(u, carry):
+        def item(i, carry):
+            zz, other, slot, fresh = pick_item(u, i)
+
+            @pl.when(jnp.logical_and(fresh, zz != end_of))
+            def _():
+                stage[slot] = project(slot, inner_w)
+                qkv_outward(slot).start()
+
+            return carry
+
+        return lax.fori_loop(0, 4, item, carry)
 
     def step(u, carry):
         for way in (0, 1):
             zz = z - u if way == 0 else z + u
-            live = inside(zz)
+            live = jnp.logical_and(inside(zz), jnp.logical_or(inner, u == 0))
+            fresh = live if way == 0 else jnp.logical_and(live, u > 0)
 
             @pl.when(jnp.logical_and(live, u > 0))
             def _():
-                w_ring(way, u - 1, zz).wait_recv()
-
-            @pl.when(jnp.logical_and(live, forwards(way)))
-            def _():
-                w_ring(way, u, zz).start()
-
-            @pl.when(jnp.logical_and(live, u > 0))
-            def _():
-                for k in range(1, n_tm):
-                    w_peer(k, zz, tm).start()
-
-        for way in (0, 1):
-            zz = z - u if way == 0 else z + u
-            live = inside(zz)
-            fresh = live if way == 0 else jnp.logical_and(live, u > 0)
-
-            @pl.when(jnp.logical_and(live, u > 0))
-            def _():
                 x_ring(way, u - 1, zz).wait_recv()
 
-            @pl.when(jnp.logical_and(live, forwards(way)))
+            @pl.when(jnp.logical_and(live, forwards_x(way)))
             def _():
                 x_ring(way, u, zz).start()
 
@@ -182,33 +244,74 @@
             def _():
                 x_sibling(zz, core).start()
 
+        @pl.when(outer)
+        def _():
+            spread_w(u)
+
         def item(i, carry):
-            way = i % 2
-            other = i // 2
-            zz = z - u + way * 2 * u
-            fresh = jnp.logical_and(inside(zz), way * (1 - jnp.minimum(u, 1)) == 0)
-
-            @pl.when(fresh)
+            zz, other, slot, fresh = pick_item(u, i)
+            here = jnp.logical_or(inner, u == 0)
+
+            @pl.when(jnp.logical_and(fresh, here))
             def _():
                 @pl.when(other == 1)
                 def _():
                     x_sibling(zz, 1 - core).wait_recv()
 
-                slot = zz * 2 + core + other * (1 - 2 * core)
-                project(slot)
-
-                @pl.when(tm > 0)
-                def _():
-                    kv_copy(0, slot).start()
-
-                @pl.when(tm < n_tm - 1)
-                def _():
-                    kv_copy(1, slot).start()
+                kv[0, rows_of(slot, tokens), 0 : 3 * hd] = project(slot, wq_ref)
+
+            @pl.when(jnp.logical_and(fresh, jnp.logical_not(here)))
+            def _():
+                qkv_outward(slot).wait_recv()
+
+            @pl.when(jnp.logical_and(fresh, tm > 0))
+            def _():
+                kv_copy(0, slot).start()
+
+            @pl.when(jnp.logical_and(fresh, tm < n_tm - 1))
+            def _():
+                kv_copy(1, slot).start()
 
             return carry
 
         lax.fori_loop(0, 4, item, 0)
+
+        @pl.when(jnp.logical_and(inner, u == 0))
+        def _():
+            wq_inward().wait_recv()
+            for k in range(1, n_tm):
+                wq_peer(k, tm).start()
+
+        @pl.when(inner)
+        def _():
+            spread_w(u)
+
+        @pl.when(jnp.logical_and(inner, u == 1))
+        def _():
+            for k in range(1, n_tm):
+                wq_peer(k, (tm + n_tm - k) % n_tm).wait_recv()
+
+        @pl.when(jnp.logical_and(inner, jnp.logical_and(u > 0, u < n_z - 1)))
+        def _():
+            lax.fori_loop((u - 1) * 2, u + 1, outward, 0)
+
         return carry
+
+    token = perm_ref[...].astype(jnp.float32)
+    rows_here, cols, plane = frame
+
+    def whole(value, by):
+        return jnp.floor((value + 0.5) * (1.0 / by))
+
+    at_frame = whole(token, plane)
+    token = token - at_frame * plane
+    row = whole(token, cols)
+    col = token - row * cols
+    shard = whole(row, rows_here)
+    pos = shard * tokens + (at_frame * rows_here + row - shard * rows_here) * cols + col
+    for i in range(group // hd):
+        block = jnp.broadcast_to(pos[:, i * hd : (i + 1) * hd], (hd, hd))
+        place[i * hd : (i + 1) * hd, :] = block.T
 
     lax.fori_loop(0, n_z, step, 0)
 
@@ -218,7 +321,7 @@
 
         @pl.when(live)
         def _():
-            kv[here, :, 2 * hd :] = jnp.ones((group, hd), jnp.bfloat16)
+            kv[here, :, 3 * hd :] = jnp.ones((group, hd), jnp.bfloat16)
 
             def arrive(slot, carry):
                 kv_copy(way, slot).wait_recv()
@@ -228,24 +331,25 @@
 
         @pl.when(jnp.logical_not(live))
         def _():
-            kv[here, :, 0:hd] = kv[0, :, 0:hd]
-            kv[here, :, hd:] = jnp.zeros((group, 2 * hd), jnp.bfloat16)
+            kv[here, :, hd : 2 * hd] = kv[0, :, hd : 2 * hd]
+            kv[here, :, 2 * hd :] = jnp.zeros((group, 2 * hd), jnp.bfloat16)
 
     factor = math.log2(math.e) * hd**-0.5
     block_rows = 2 * tokens
 
     def attend_block(i, carry):
         zz = (z + 1 + i) % n_z
-        pos = pos_ref[rows_of(zz, block_rows), :]
-        lanes = lax.broadcasted_iota(jnp.int32, (block_rows, group), 1)
-        pick = jnp.where(lanes == pos, 1.0, 0.0).astype(jnp.bfloat16)
-        query = jnp.dot(pick, queries[...], preferred_element_type=jnp.float32)
+        pos = place[rows_of(zz, block_rows), :]
+        lanes = lax.broadcasted_iota(jnp.int32, (block_rows, hd), 1).astype(jnp.float32)
+        picks = [jnp.where(pos - i * hd == lanes, 1.0, 0.0) for i in range(group // hd)]
+        pick = jnp.concatenate([p.astype(jnp.bfloat16) for p in picks], axis=1)
+        query = jnp.dot(pick, kv[0, :, 0:hd], preferred_element_type=jnp.float32)
         query = query.astype(jnp.bfloat16)
         highest = None
         for part in range(3):
             score = lax.dot_general(
                 query,
-                kv[part, :, 0:hd],
+                kv[part, :, hd : 2 * hd],
                 (((1,), (1,)), ((), ())),
                 preferred_element_type=jnp.float32,
             )
@@ -255,7 +359,7 @@
         total = jnp.zeros((block_rows, 2 * hd), jnp.float32)
         for part in range(3):
             weights = jnp.exp2((scores[part] - highest) * factor).astype(jnp.bfloat16)
-            total += jnp.dot(weights, kv[part, :, hd:], preferred_element_type=jnp.float32)
+            total += jnp.dot(weights, kv[part, :, 2 * hd :], preferred_element_type=jnp.float32)
         result = (total[:, :hd] / total[:, hd:]).astype(jnp.bfloat16)
 
         @pl.when(zz == z)
@@ -319,18 +423,40 @@
 
     lax.fori_loop(0, shards, drain, 0)
     for zz in range(n_z):
-        x_sibling(zz, core).wait_send()
+
+        @pl.when(jnp.logical_or(inner, zz == z))
+        def _():
+            x_sibling(zz, core).wait_send()
+
+        @pl.when(jnp.logical_and(inner, zz != end_of))
+        def _():
+            for side in (0, 1):
+                qkv_outward(zz * 2 + side).wait_send()
     for u in range(n_z - 1):
         for way in (0, 1):
             zz = z - u if way == 0 else z + u
 
-            @pl.when(jnp.logical_and(inside(zz), forwards(way)))
+            @pl.when(jnp.logical_and(inside(zz), forwards_w(way)))
             def _():
                 w_ring(way, u, zz).wait_send()
+
+            live = jnp.logical_and(inside(zz), jnp.logical_or(inner, u == 0))
+
+            @pl.when(jnp.logical_and(live, forwards_x(way)))
+            def _():
                 x_ring(way, u, zz).wait_send()
 
-
-def fused(n_tm, n_z, x, wq, wo, q_gain, k_gain, pos):
+    @pl.when(outer)
+    def _():
+        wq_inward().wait_send()
+
+    @pl.when(inner)
+    def _():
+        for k in range(1, n_tm):
+            wq_peer(k, tm).wait_send()
+
+
+def fused(n_tm, n_z, frame, x, wq, wo, q_gain, k_gain, perm):
     tokens, model = x.shape
     hd = wo.shape[0]
     shards = 2 * n_z
@@ -339,15 +465,17 @@
     dma = pltpu.SemaphoreType.DMA
     vmem = pl.BlockSpec(memory_space=pltpu.VMEM)
     return pl.pallas_call(
-        functools.partial(fused_kernel, n_tm, n_z),
+        functools.partial(fused_kernel, n_tm, n_z, frame),
         out_shape=jax.ShapeDtypeStruct((tokens, model), bf),
         in_specs=[vmem] * 6,
         out_specs=vmem,
         scratch_shapes=[
             pltpu.VMEM((shards, tokens, model), bf),
             pltpu.VMEM((n_tm, n_z * hd, model // n_tm), bf),
-            pltpu.VMEM((group, hd), bf),
-            pltpu.VMEM((3, group, 3 * hd), bf),
+            pltpu.VMEM((model, 3 * hd), bf),
+            pltpu.VMEM((shards, tokens, 3 * hd), bf),
+            pltpu.VMEM((group, hd), jnp.float32),
+            pltpu.VMEM((3, group, 4 * hd), bf),
             pltpu.VMEM((3, 2 * tokens, group), jnp.float32),
             pltpu.VMEM((n_z, 2 * tokens, hd), bf),
             pltpu.VMEM((n_z, 2 * tokens, hd), bf),
@@ -367,11 +495,17 @@
             dma((n_z,)),
             dma((n_tm,)),
             dma((n_tm,)),
+            dma,
+            dma,
+            dma((n_tm - 1,)),
+            dma((n_tm - 1,)),
+            dma((shards,)),
+            dma((shards,)),
         ],
         compiler_params=pltpu.CompilerParams(
             collective_id=0, has_side_effects=True, vmem_limit_bytes=56 * 1024 * 1024
         ),
-    )(x, wq, wo, q_gain, k_gain, pos)
+    )(x, wq, wo, q_gain, k_gain, perm)
 
 
 def whole_window(video, w_qkv, w_out, q_gain, k_gain, tile_perm):
@@ -379,22 +513,17 @@
     n_tm = lax.axis_size("tm")
     n_space = lax.axis_size("space")
     hd = w_out.shape[1]
-    place = tile_perm[0]
-    rows = rows_here * n_space
-    frame = place // (rows * cols)
-    row = place // cols % rows
-    col = place % cols
     tokens = frames * rows_here * cols
-    pos = (row // rows_here) * tokens + (frame * rows_here + row % rows_here) * cols + col
     mixed = fused(
         n_tm,
         n_space // 2,
+        (rows_here, cols, rows_here * n_space * cols),
         video.reshape(tokens, model),
         w_qkv.reshape(model, 3 * hd),
         w_out.reshape(hd, model),
         q_gain.reshape(1, hd),
         k_gain.reshape(1, hd),
-        pos.reshape(-1, 1),
+        tile_perm,
     )
     return mixed[None]
 
@@ -442,7 +571,8 @@
 
 def per_device(video, w_qkv, w_out, q_gain, k_gain, tile_perm, window):
     tiles = video.shape[0] * video.shape[1] * lax.axis_size("space") * video.shape[2] // (TT * TH * TW)
-    if window.shape[1] == tiles and w_qkv.shape[1] == 1:
+    sized = lax.axis_size("tm") == 4 and lax.axis_size("space") == 8
+    if window.shape[1] == tiles and w_qkv.shape[1] == 1 and sized:
         return whole_window(video, w_qkv, w_out, q_gain, k_gain, tile_perm)
     frames_here = video.shape[0]
     cols_here = video.shape[2]

time: 143 us -> 133 us (0.930)
  Pallas kernels: 135 us -> 130 us
  other arithmetic: 3.89 us -> 0 us
  local copies, waits for them, and re-layouts: 4.02 us -> 2.36 us
    pallas_call x1, Pallas kernels: 135 us -> 130 us  [fused(): pl.pallas_call(functools.partial(fused_kernel, n_tm, n_z, frame), out_sha...]
    add x1 -> x0, other arithmetic: 2.43 us -> none  [whole_window(): row // rows_here * tokens + (frame * rows_here + row % rows_here) * cols]
where the time goes in v2:
time: 133 us; the launch traced here: 132 us
  Pallas kernels  130 us (98%)
  local copies, waits for them, and re-layouts  2.36 us (2%)
    pallas_call x1, Pallas kernels, fused(): pl.pallas_call(functools.partial(fused_kernel, n_tm, n_z, frame), out_sha...  130 us

profile of v2, /device:TPU:5, one launch (start us, length us, event | category | flops | bytes accessed | tf_op | source)
XLA Modules:
  0.0 132.0 jit_solution(4192830247388535554)
XLA Ops:
  0.0 129.6 %shard_map.64 = bf16[192,3072]{1,0:T(8,128)(2,1)} custom-call(bf16[192,3072]{1,0:T(8,128)(2,1)} %bitcast.8, bf16[3072,384]{1,0:T(8,128)(2,1)} %bitcast.7, bf16[128,3072]{1,0:T(8,128)(2,1)} %bitcast.9, f32[1,128]{1,0:T(1,128)} %bitcast.10, f32[1,128]{1,0:T(1,128)} %bitcast.11, s32[1,1536]{1,0:T(1,128)} %perm_ref.1), custom_call_target="tpu_custom_call" | custom-call | tf_op jit(solution)/shard_map/pallas_call | solution.py:467
  129.6 2.4 %copy.8 = bf16[1,192,3072]{2,1,0:T(8,128)(2,1)} copy(bf16[1,192,3072]{2,1,0:T(8,128)(2,1)} %bitcast.6) | data formatting | bytes 2359296
